TPU v7x, 512 devices: a whole 4x4x16 slice. The times are simulated.
512 devices in a mesh: ctx: 128 (over y, z, core), head: 4 (over x).
Axes of the slice: x: 4, y: 4, z: 16, core: 2. Of those that a mesh axis runs over, the one named last changes fastest.
Arguments:
- queries: bfloat16 [32768, 2048], P('ctx', 'head'), may hold values from -16 to 16
- key_rows: bfloat16 [32768, 512], P('ctx', 'head'), may hold values from -16 to 16
- value_rows: bfloat16 [32768, 512], P('ctx', 'head'), may hold values from -6 to 6
- vertical_rows: int32 [8192, 4], P(None, 'head'), may hold values from 0 to 255, as said below
- slash_offsets: int32 [8, 4], P(None, 'head'), may hold values from 1 to 127
- block_mask: int32 [512, 2, 4], P('ctx', None, 'head'), may hold values 0 or 1
Outputs:
- attended: bfloat16 [32768, 2048], P(('ctx', 'head'))
Inputs may be any that keep to these rules, and one draw needn't show every extreme that they name: `vertical_rows`: within each aligned block of 64 rows the entries of one column are distinct.
All inputs are finite; a program needn't handle non-finite values. No bound on the sum of `block_mask` on one device may be relied on, other than what follows from the above.
Results may differ from a plain program's by a relative error of at most 0.009.
Values may be sent and summed in bfloat16 or wider, within the bound.
A program may use at most 128 MiB of HBM per device.

v0:
```python
import math

import jax
import jax.numpy as jnp
from jax import lax
from jax.sharding import PartitionSpec as P

HD = 128
BLK = 64
VB = 64
HALF = 128


def placed(owner_ids, local_rows, ctx_count):
    return jnp.where(
        local_rows < HALF,
        owner_ids * HALF + local_rows,
        (2 * ctx_count - 1 - owner_ids) * HALF + local_rows - HALF,
    )


def local_allowed(positions, local_rows, mask_rows, slash):
    query_pos = positions[:, None]
    key_pos = positions[None, :]
    same_half = query_pos // HALF == key_pos // HALF
    causal = key_pos <= query_pos
    same_block = query_pos // BLK == key_pos // BLK
    offset = query_pos - key_pos
    slash_hit = jnp.any(offset[None, None] == jnp.transpose(slash)[:, :, None, None], axis=1)
    block_bits = mask_rows[local_rows // BLK][:, positions % HALF // BLK]
    block_hit = jnp.transpose(block_bits, (2, 0, 1)) == 1
    return same_half[None] & causal[None] & (same_block[None] | slash_hit | block_hit)


def on_device(queries, key_rows, value_rows, vertical_rows, slash_offsets, block_mask):
    row_count = queries.shape[0]
    kv_heads = key_rows.shape[1] // HD
    group_size = queries.shape[1] // key_rows.shape[1]
    ctx_count = lax.axis_size("ctx")
    ctx_index = lax.axis_index("ctx")
    head_count = lax.axis_size("head")
    score_scale = HD ** (-0.5)
    local_rows = jnp.arange(row_count, dtype=jnp.int32)
    positions = placed(ctx_index, local_rows, ctx_count)
    half_start = positions - positions % HALF
    query_tiles = queries.reshape(row_count, kv_heads, group_size, HD)
    key_tiles = key_rows.reshape(row_count, kv_heads, HD)
    value_tiles = value_rows.reshape(row_count, kv_heads, HD)
    allowed = local_allowed(positions, local_rows, block_mask, slash_offsets)
    local_scores = (
        jnp.einsum("tkgd,skd->kgts", query_tiles, key_tiles, preferred_element_type=jnp.float32)
        * score_scale
    )
    local_scores = jnp.where(allowed[:, None], local_scores, -jnp.inf)
    running_max = jnp.max(local_scores, axis=3)
    local_weights = jnp.exp(local_scores - running_max[..., None])
    weight_sum = jnp.sum(local_weights, axis=3)
    numerator = jnp.einsum("kgts,skd->kgtd", local_weights, value_tiles.astype(jnp.float32))
    own_lines = lax.dynamic_slice_in_dim(vertical_rows, ctx_index * VB, VB, 0)
    gather_index = jnp.broadcast_to(own_lines[:, :, None], (VB, kv_heads, HD))
    line_keys = jnp.take_along_axis(key_tiles, gather_index, axis=0).reshape(VB, kv_heads * HD)
    line_values = jnp.take_along_axis(value_tiles, gather_index, axis=0).reshape(VB, kv_heads * HD)

    def absorb(softmax_state, pieces, first_row):
        peak_now, sum_now, numer_now = softmax_state
        piece_keys = pieces[0].reshape(-1, kv_heads, HD)
        piece_values = pieces[1].reshape(-1, kv_heads, HD)
        piece_rows = piece_keys.shape[0]
        line_index = lax.dynamic_slice_in_dim(vertical_rows, first_row, piece_rows, 0)
        owner_ids = (first_row + jnp.arange(piece_rows, dtype=jnp.int32)) // VB
        line_pos = placed(owner_ids[:, None], line_index, ctx_count)
        visible = jnp.transpose(line_pos)[:, None, :] < half_start[None, :, None]
        scores = (
            jnp.einsum(
                "tkgd,nkd->kgtn", query_tiles, piece_keys, preferred_element_type=jnp.float32
            )
            * score_scale
        )
        scores = jnp.where(visible[:, None], scores, -jnp.inf)
        new_peak = jnp.maximum(peak_now, jnp.max(scores, axis=3))
        rescale = jnp.exp(peak_now - new_peak)
        weights = jnp.exp(scores - new_peak[..., None])
        new_sum = sum_now * rescale + jnp.sum(weights, axis=3)
        new_numer = numer_now * rescale[..., None] + jnp.einsum(
            "kgtn,nkd->kgtd", weights, piece_values.astype(jnp.float32)
        )
        return (new_peak, new_sum, new_numer)

    softmax_state = (running_max, weight_sum, numerator)
    gathered = (
        lax.all_gather(line_keys, "ctx", axis=0, tiled=True),
        lax.all_gather(line_values, "ctx", axis=0, tiled=True),
    )
    line_total = gathered[0].shape[0]
    block_rows = math.gcd(line_total, 2048)
    block_count = line_total // block_rows
    stacked_keys = gathered[0].reshape(block_count, block_rows, -1)
    stacked_values = gathered[1].reshape(block_count, block_rows, -1)

    def absorb_block(state_now, block_item):
        block_number, block_keys, block_values = block_item
        return (absorb(state_now, (block_keys, block_values), block_number * block_rows), None)

    softmax_state, _ = lax.scan(
        absorb_block,
        softmax_state,
        (jnp.arange(block_count, dtype=jnp.int32), stacked_keys, stacked_values),
    )
    final_peak, final_sum, final_numer = softmax_state
    result = final_numer / final_sum[..., None]
    result = jnp.transpose(result, (2, 0, 1, 3)).reshape(row_count, -1).astype(jnp.bfloat16)
    head_cols = result.shape[1]
    quarter = row_count // head_count
    stacked = result.reshape(head_count, quarter, head_cols)
    arrived = lax.all_to_all(stacked, "head", split_axis=0, concat_axis=0, tiled=True)
    return jnp.transpose(arrived, (1, 0, 2)).reshape(quarter, head_count * head_cols)


def solution(mesh):
    placed = (
        P("ctx", "head"),
        P("ctx", "head"),
        P("ctx", "head"),
        P(None, "head"),
        P(None, "head"),
        P("ctx", None, "head"),
    )
    return jax.shard_map(
        on_device, mesh=mesh, in_specs=placed, out_specs=P(("ctx", "head"), None), check_vma=False
    )
```

profile of v0, /device:TPU:1, one launch (start us, length us, event | category | flops | bytes accessed | tf_op | source)
XLA Modules:
  0.0 483.1 jit_solution(8751360739792305288)
XLA Ops:
  6.5 0.0 copy-start
  6.5 0.0 all-gather.5.cloned.1.call-start
  6.5 0.8 broadcast_compare_fusion.1
  7.3 0.1 fusion.43
  7.4 0.0 copy-done
  7.4 0.0 copy-start.1
  7.4 65.6 %gather_fusion.2 = bf16[8192]{0:T(1024)(128)(2,1)S(1)} fusion(bf16[256,128]{1,0:T(8,128)(2,1)S(1)} %copy-done, s32[8192]{0:T(1024)S(1)} %fusion.43), kind=kCustom, calls=%fused_computation.clone | custom fusion | bytes 98304 | tf_op jit(solution)/shard_map/jit(take_along_axis)/gather | solution.py:61
  73.1 0.0 copy-done.1
  73.1 0.0 copy-start.4
  73.1 0.0 copy-start.3
  73.1 0.0 copy-start.2
  73.1 65.6 %gather_fusion.3 = bf16[8192]{0:T(1024)(128)(2,1)S(1)} fusion(bf16[256,128]{1,0:T(8,128)(2,1)S(1)} %copy-done.1, s32[8192]{0:T(1024)S(1)} %fusion.43), kind=kCustom, calls=%fused_computation.1.clone | custom fusion | bytes 98304 | tf_op jit(solution)/shard_map/jit(take_along_axis)/gather | solution.py:62
  138.8 0.7 bitcast_select_fusion.2
  139.5 0.0 all-gather.5.cloned.1.call-update
  139.5 0.0 all-gather.7.cloned.1.call-start
  139.6 0.7 all-gather.7.cloned.1.call-update
  140.3 0.1 broadcast_subtract_fusion
  140.4 0.1 copy.33
  140.5 0.0 copy-done.4
  140.5 0.3 compare_reduce_fusion
  140.9 0.2 copy.34
  141.1 0.1 copy.35
  141.2 0.7 gather_fusion
  141.9 0.1 copy.36
  142.0 0.0 copy-done.2
  142.0 0.1 copy.39
  142.1 0.2 copy.40
  142.4 1.0 gather_fusion.1
  143.4 0.2 fusion.37
  143.5 0.3 fusion.46
  143.9 0.2 fusion.32
  144.0 0.3 convolution_bitcast_fusion
  144.4 140.9 %all-gather.5.cloned.1.call-done = bf16[8192,1,128]{2,0,1:T(8,128)(2,1)} async-done(((bf16[64,1,128]{2,0,1:T(8,128)(2,1)}), bf16[8192,1,128]{2,0,1:T(8,128)(2,1)}) %all-gather.5.cloned.1.call-update) | async-done | bytes 2097168 | tf_op jit(solution)/shard_map/all_gather | solution.py:91
  285.2 139.2 %all-gather.7.cloned.1.call-done = bf16[8192,1,128]{2,0,1:T(8,128)(2,1)} async-done(((bf16[64,1,128]{2,0,1:T(8,128)(2,1)}), bf16[8192,1,128]{2,0,1:T(8,128)(2,1)}) %all-gather.7.cloned.1.call-update) | async-done | bytes 2097168 | tf_op jit(solution)/shard_map/all_gather | solution.py:92
  424.4 40.6 %while.17 = (s32[]{:T(128)}, f32[1,4,256]{2,1,0:T(4,128)S(1)}, f32[1,4,256]{2,1,0:T(4,128)S(1)}, f32[1,4,256,128]{3,2,1,0:T(8,128)S(1)}, s32[4]{0:T(128)S(1)}, /...) while((s32[]{:T(128)}, f32[1,4,256]{2,1,0:T(4,128)S(1)}, ...), condition=%wide.region_6.8_spmd.clone, body=%wide.region_3.7_spmd.clone.sunk | while | flops 1095556352 | bytes 29715672 | solution.py:104
  424.4 0.6 dynamic_slice.54
  425.7 0.8 compare_select_fusion.17
  426.4 0.5 broadcast_compare_fusion.3
  426.9 2.4 fusion.58
  429.4 3.3 fusion.61
  432.7 1.8 fusion.60
  434.6 0.6 dynamic_slice.54
  435.8 0.8 compare_select_fusion.17
  436.6 0.5 broadcast_compare_fusion.3
  437.1 2.4 fusion.58
  439.5 3.3 fusion.61
  442.8 1.8 fusion.60
  444.7 0.6 dynamic_slice.54
  446.0 0.8 compare_select_fusion.17
  446.7 0.5 broadcast_compare_fusion.3
  447.2 2.4 fusion.58
  449.7 3.3 fusion.61
  453.0 1.8 fusion.60
  454.9 0.6 dynamic_slice.54
  456.1 0.8 compare_select_fusion.17
  456.9 0.5 broadcast_compare_fusion.3
  457.4 2.4 fusion.58
  459.8 3.3 fusion.61
  463.2 1.8 fusion.60
  465.0 0.2 fusion.36
  465.2 0.2 copy.41
  465.5 0.1 convert_element_type.14
  465.6 10.0 %all_to_all.5 = bf16[4,64,512]{2,1,0:T(8,128)(2,1)S(1)} all-to-all(bf16[4,64,512]{2,1,0:T(8,128)(2,1)S(1)} %convert_element_type.14), channel_id=1, replica_groups=mesh['ctx'=128,'head'=4] {'head'}, dimensions={0} | all-to-all | bytes 524288 | tf_op jit(solution)/shard_map/all_to_all | solution.py:115
  475.6 0.7 copy.46
  (25 shorter events, 0.2 us)
Async XLA Ops:
  6.5 0.9 copy-start
  6.5 278.7 %all-gather.5.cloned.1.call-start = ((), (), s32[]{:S(2)}) async-start(), calls=%async_computation.1 | async-start | bytes 2113536 | tf_op jit(solution)/shard_map/all_gather | solution.py:91
  7.4 65.7 %copy-start.1 = (bf16[256,128]{1,0:T(8,128)(2,1)S(1)}, bf16[256,128]{1,0:T(8,128)(2,1)}, u32[]{:S(2)}) copy-start(bf16[256,128]{1,0:T(8,128)(2,1)} %param.12) | copy-start | bytes 196612
  73.1 67.4 %copy-start.4 = (s32[8,1]{0,1:T(1,128)S(1)}, s32[8,1]{0,1:T(1,128)}, u32[]{:S(2)}) copy-start(s32[8,1]{0,1:T(1,128)} %param.14) | copy-start | bytes 100
  73.1 67.9 %copy-start.3 = (s32[4,2,1]{0,2,1:T(1,128)S(1)}, s32[4,2,1]{0,2,1:T(1,128)}, u32[]{:S(2)}) copy-start(s32[4,2,1]{0,2,1:T(1,128)} %param.15) | copy-start | bytes 100
  73.1 68.9 %copy-start.2 = (bf16[256,512]{1,0:T(8,128)(2,1)S(1)}, bf16[256,512]{1,0:T(8,128)(2,1)}, u32[]{:S(2)}) copy-start(bf16[256,512]{1,0:T(8,128)(2,1)} %param.10) | copy-start | bytes 786436
  139.5 284.9 %all-gather.7.cloned.1.call-start = ((), (), s32[]{:S(2)}) async-start(), calls=%async_computation.2 | async-start | bytes 2113536 | tf_op jit(solution)/shard_map/all_gather | solution.py:92
Sparse Core Ops, SparseCore 0:
  139.6 145.5 all-gather.4
  288.4 135.9 all-gather.6
where the time goes:
time: 484 us; the launch traced here: 483 us
  waiting for transfers between devices  281 us (58%)
  local copies, waits for them, and re-layouts  137 us (28%)
  matrix products  23.7 us (5%)
  other arithmetic  15 us (3%)
  between operations  13.6 us (3%)
  blocking collectives  10 us (2%)
    all_gather x1, waiting for transfers between devices, on_device(): lax.all_gather(line_keys, 'ctx', axis=0, tiled=True)  141 us
    all_gather x1, waiting for transfers between devices, on_device(): lax.all_gather(line_values, 'ctx', axis=0, tiled=True)  139 us
    gather x1, local copies, waits for them, and re-layouts, on_device(): jnp.take_along_axis(key_tiles, gather_index, axis=0)  65.6 us
    gather x1, local copies, waits for them, and re-layouts, on_device(): jnp.take_along_axis(value_tiles, gather_index, axis=0)  65.6 us
    dot_general x4, matrix products, absorb(): jnp.einsum('kgtn,nkd->kgtd', weights, piece_values.astype(jnp.float32))  13.3 us
    all_to_all x1, blocking collectives, on_device(): lax.all_to_all(stacked, 'head', split_axis=0, concat_axis=0, tiled=True)  10 us
    dot_general x4, matrix products, absorb(): jnp.einsum('tkgd,nkd->kgtn', query_tiles, piece_keys, preferred_element_t...  9.73 us
  transfers between devices with their start and end apart: 2, of which 2 were waited for; matrix products, arithmetic and copies ran while one was open for 1% of the time, Pallas kernels for 0%

commit v1 on v0

v1 whole, which is shorter than its diff:
```python
import math

import jax
import jax.numpy as jnp
from jax import lax
from jax.experimental import pallas as pl
from jax.experimental.pallas import tpu as pltpu
from jax.sharding import PartitionSpec as P

HD = 128
BLK = 64
VB = 64
HALF = 128
NY = 4
NZ = 16
NC = 2
GROUP = 4
NEG = -1e30
SCALE = HD**-0.5 * math.log2(math.e)
MESH = pl.DeviceIdType.MESH


def kernel(
    q_hbm, k_hbm, v_hbm, vr_hbm, slash_ref, bm_ref, out_hbm,
    q_ref, k_ref, v_ref, vr_ref, lines, peak, acc, res,
    in_sem, y_send, y_recv, up_send, up_recv, dn_send, dn_recv,
    su_send, su_recv, sd_send, sd_recv, x_send, x_recv, own_sem,
):
    c = lax.axis_index("ctx")
    h = lax.axis_index("head")
    heads = lax.axis_size("head")
    y = c // (NZ * NC)
    z = (c // NC) % NZ
    core = c % NC

    def dev(yy, zz, cc):
        return (yy * (NZ * NC) + zz * NC + cc, h)

    sibling = dev(y, z, 1 - core)
    z_up = dev(y, (z + 1) % NZ, core)
    z_dn = dev(y, (z + NZ - 1) % NZ, core)

    loads = [
        pltpu.make_async_copy(src, dst, in_sem.at[i])
        for i, (src, dst) in enumerate(
            ((vr_hbm, vr_ref), (k_hbm, k_ref), (v_hbm, v_ref), (q_hbm, q_ref))
        )
    ]
    for load in loads:
        load.start()

    barrier = pltpu.get_barrier_semaphore()
    greeted = [sibling, z_up, z_dn]
    greeted += [dev((y + d) % NY, z, core) for d in (1, 2, 3)]
    greeted += [(c, (h + d) % heads) for d in (1, 2, 3)]
    for who in greeted:
        pl.semaphore_signal(barrier, inc=1, device_id=who, device_id_type=MESH)

    for load in loads[:3]:
        load.wait()
    chip_rows = vr_ref[y, pl.ds(z, 1), :]
    picks = lax.broadcasted_iota(jnp.int32, (2 * HALF, NC * VB), 0) == chip_rows
    picks = jnp.where(picks, 1.0, 0.0).astype(jnp.bfloat16)
    for kv, src in ((0, k_ref), (1, v_ref)):
        both = lax.dot_general(
            picks, src[...], (((0,), (0,)), ((), ())), preferred_element_type=jnp.float32
        ).astype(jnp.bfloat16)
        for cc in range(NC):
            @pl.when(core == cc)
            def _():
                lines[z, kv, y, cc] = both[cc * VB : (cc + 1) * VB]

    pl.semaphore_wait(barrier, len(greeted))

    def y_copy(d):
        block = lines.at[z, :, y, core]
        return pltpu.make_async_remote_copy(
            block, block, y_send.at[d - 1], y_recv.at[d - 1],
            device_id=dev((y + d) % NY, z, core), device_id_type=MESH,
        )

    for d in (1, 2, 3):
        y_copy(d).start()
    loads[3].wait()

    def z_copy(s, zz, upward):
        block = lines.at[zz, :, :, core]
        if upward:
            return pltpu.make_async_remote_copy(
                block, block, up_send.at[s], up_recv.at[s], device_id=z_up, device_id_type=MESH
            )
        return pltpu.make_async_remote_copy(
            block, block, dn_send.at[s], dn_recv.at[s], device_id=z_dn, device_id_type=MESH
        )

    def last_copy(zz, upward):
        kv = 0 if upward else 1
        block = lines.at[zz, kv, :, core]
        if upward:
            return pltpu.make_async_remote_copy(
                block, block, up_send.at[8], up_recv.at[8], device_id=z_up, device_id_type=MESH
            )
        return pltpu.make_async_remote_copy(
            block, block, dn_send.at[8], dn_recv.at[8], device_id=z_dn, device_id_type=MESH
        )

    def sib_copy(s, zz, upward, who):
        block = lines.at[zz, :, :, who]
        send, recv = (su_send, su_recv) if upward else (sd_send, sd_recv)
        return pltpu.make_async_remote_copy(
            block, block, send.at[s], recv.at[s], device_id=sibling, device_id_type=MESH
        )

    ones = jnp.ones((NY * NC * VB, HD), jnp.bfloat16)

    def queries_of(half):
        return jnp.concatenate(
            [
                q_ref[half * HALF : (half + 1) * HALF, g * HD : (g + 1) * HD]
                for g in range(GROUP)
            ],
            axis=0,
        )

    qi = lax.broadcasted_iota(jnp.int32, (HALF, HALF), 0)
    kj = lax.broadcasted_iota(jnp.int32, (HALF, HALF), 1)
    offset = qi - kj
    slash_hit = offset == slash_ref[0]
    for n in range(1, slash_ref.shape[0]):
        slash_hit = slash_hit | (offset == slash_ref[n])
    base = (qi // BLK == kj // BLK) | slash_hit
    for half in range(2):
        bits = [
            [jnp.full((HALF, HALF), bm_ref[kb, 2 * half + qb], jnp.int32) for kb in range(2)]
            for qb in range(2)
        ]
        top = jnp.where(kj < BLK, bits[0][0], bits[0][1])
        low = jnp.where(kj < BLK, bits[1][0], bits[1][1])
        hit = jnp.where(qi < BLK, top, low) == 1
        allowed = (kj <= qi) & (base | hit)
        bias = jnp.where(allowed, 0.0, NEG)
        rows = slice(half * HALF, (half + 1) * HALF)
        s = lax.dot_general(
            queries_of(half), k_ref[rows, :], (((1,), (1,)), ((), ())),
            preferred_element_type=jnp.float32,
        )
        s = s + jnp.concatenate([bias] * GROUP, axis=0)
        top_score = jnp.broadcast_to(jnp.max(s, axis=1, keepdims=True), s.shape)
        peak[half] = top_score
        weights = jnp.exp2((s - top_score) * SCALE).astype(jnp.bfloat16)
        vals = jnp.concatenate([v_ref[rows, :], ones[:HALF]], axis=1)
        acc[half] = jnp.dot(weights, vals, preferred_element_type=jnp.float32)

    lane = lax.broadcasted_iota(jnp.int32, (1, NC * VB), 1)

    def absorb(zz):
        low_bias, high_bias = [], []
        for yy in range(NY):
            is_low = vr_ref[yy, pl.ds(zz, 1), :] < HALF
            owner = yy * (NZ * NC) + zz * NC + lane // VB
            low_bias.append(jnp.where(is_low & (owner < c), 0.0, NEG))
            high_bias.append(jnp.where(is_low | (owner > c), 0.0, NEG))
        keys = lines[zz, 0].reshape(NY * NC * VB, HD)
        vals = jnp.concatenate([lines[zz, 1].reshape(NY * NC * VB, HD), ones], axis=1)
        for half, parts in ((0, low_bias), (1, high_bias)):
            bias = jnp.concatenate(parts, axis=1)
            s = lax.dot_general(
                queries_of(half), keys, (((1,), (1,)), ((), ())),
                preferred_element_type=jnp.float32,
            )
            s = s + bias
            old = peak[half]
            new = jnp.maximum(old, jnp.max(s, axis=1, keepdims=True))
            peak[half] = new
            weights = jnp.exp2((s - jnp.concatenate([new] * NY, axis=1)) * SCALE)
            rescale = jnp.exp2((old - new) * SCALE)
            acc[half] = acc[half] * jnp.concatenate([rescale] * 2, axis=1) + jnp.dot(
                weights.astype(jnp.bfloat16), vals, preferred_element_type=jnp.float32
            )

    for d in (1, 2, 3):
        y_copy(d).wait_recv()
    z_copy(1, z, True).start()
    z_copy(1, z, False).start()
    sib_copy(0, z, True, core).start()

    sib_copy(0, z, True, 1 - core).wait_recv()
    absorb(z)

    def step(s, carry):
        for upward in (True, False):
            zz = (z + NZ - s) % NZ if upward else (z + s) % NZ
            z_copy(s, zz, upward).wait_recv()
            @pl.when(s < 7)
            def _():
                z_copy(s + 1, zz, upward).start()
            @pl.when(s == 7)
            def _():
                last_copy(zz, upward).start()
            sib_copy(s, zz, upward, core).start()
            @pl.when(s > 1)
            def _():
                before = (z + NZ - s + 1) % NZ if upward else (z + s - 1) % NZ
                sib_copy(s - 1, before, upward, 1 - core).wait_recv()
                absorb(before)
        return carry

    lax.fori_loop(1, 8, step, 0)
    far = (z + 8) % NZ
    last_copy(far, True).wait_recv()
    last_copy(far, False).wait_recv()
    sib_copy(8, far, True, core).start()
    for upward in (True, False):
        before = (z + NZ - 7) % NZ if upward else (z + 7) % NZ
        sib_copy(7, before, upward, 1 - core).wait_recv()
        absorb(before)
    sib_copy(8, far, True, 1 - core).wait_recv()
    absorb(far)

    quarter = res.shape[0] // 4
    cols = GROUP * HD

    def x_copy(d):
        to = (h + d) % heads
        return pltpu.make_async_remote_copy(
            res.at[pl.ds(to * quarter, quarter), :],
            out_hbm.at[:, pl.ds(pl.multiple_of(h * cols, cols), cols)],
            x_send.at[d - 1], x_recv.at[d - 1],
            device_id=(c, to), device_id_type=MESH,
        )

    for half in range(2):
        total = acc[half]
        done = (total[:, :HD] / total[:, HD:]).astype(jnp.bfloat16)
        for g in range(GROUP):
            res[half * HALF : (half + 1) * HALF, g * HD : (g + 1) * HD] = done[
                g * HALF : (g + 1) * HALF
            ]
    own = pltpu.make_async_copy(
        res.at[pl.ds(h * quarter, quarter), :],
        out_hbm.at[:, pl.ds(pl.multiple_of(h * cols, cols), cols)],
        own_sem,
    )
    own.start()
    for d in (2, 1, 3):
        x_copy(d).start()

    for d in (1, 2, 3):
        y_copy(d).wait_send()
    sib_copy(0, z, True, core).wait_send()

    def drain(s, carry):
        for upward in (True, False):
            zz = (z + NZ - s) % NZ if upward else (z + s) % NZ
            z_copy(s, zz, upward).wait_send()
            sib_copy(s, zz, upward, core).wait_send()
        return carry

    lax.fori_loop(1, 8, drain, 0)
    last_copy(far, True).wait_send()
    last_copy(far, False).wait_send()
    sib_copy(8, far, True, core).wait_send()
    own.wait()
    for d in (1, 2, 3):
        x_copy(d).wait_send()
    for d in (1, 2, 3):
        x_copy(d).wait_recv()


def on_device(queries, key_rows, value_rows, vertical_rows, slash_offsets, block_mask):
    rows = queries.shape[0]
    heads = lax.axis_size("head")
    cols = queries.shape[1]
    dma = pltpu.SemaphoreType.DMA
    return pl.pallas_call(
        kernel,
        out_shape=jax.ShapeDtypeStruct((rows // heads, heads * cols), jnp.bfloat16),
        in_specs=[pl.BlockSpec(memory_space=pl.ANY)] * 4
        + [pl.BlockSpec(memory_space=pltpu.SMEM)] * 2,
        out_specs=pl.BlockSpec(memory_space=pl.ANY),
        scratch_shapes=[
            pltpu.VMEM((rows, cols), jnp.bfloat16),
            pltpu.VMEM((rows, HD), jnp.bfloat16),
            pltpu.VMEM((rows, HD), jnp.bfloat16),
            pltpu.VMEM((NY, NZ, NC * VB), jnp.int32),
            pltpu.VMEM((NZ, 2, NY, NC, VB, HD), jnp.bfloat16),
            pltpu.VMEM((2, GROUP * HALF, HD), jnp.float32),
            pltpu.VMEM((2, GROUP * HALF, 2 * HD), jnp.float32),
            pltpu.VMEM((rows, cols), jnp.bfloat16),
            dma((4,)),
            dma((3,)), dma((3,)),
            dma((9,)), dma((9,)), dma((9,)), dma((9,)),
            dma((9,)), dma((9,)), dma((9,)), dma((9,)),
            dma((3,)), dma((3,)),
            dma,
        ],
        compiler_params=pltpu.CompilerParams(
            collective_id=0, has_side_effects=True, vmem_limit_bytes=48 * 1024 * 1024
        ),
        cost_estimate=pl.CostEstimate(
            flops=4 * 1024 * 8192 * HD, bytes_accessed=2**20, transcendentals=1024 * 8192
        ),
    )(
        queries, key_rows, value_rows,
        vertical_rows.reshape(NY, NZ, NC * VB),
        slash_offsets.reshape(-1),
        jnp.transpose(block_mask, (1, 2, 0)).reshape(2, -1),
    )


def solution(mesh):
    placed = (
        P("ctx", "head"),
        P("ctx", "head"),
        P("ctx", "head"),
        P(None, "head"),
        P(None, "head"),
        P("ctx", None, "head"),
    )
    return jax.shard_map(
        on_device, mesh=mesh, in_specs=placed, out_specs=P(("ctx", "head"), None), check_vma=False
    )
```

time: 484 us -> 68.6 us (0.14)
  waiting for transfers between devices: 281 us -> 0 us
  local copies, waits for them, and re-layouts: 137 us -> 4.77 us
  Pallas kernels: 0 us -> 63.5 us
  matrix products: 23.7 us -> 0 us
  other arithmetic: 15 us -> 0 us
  between operations: 13.6 us -> 0.02 us
  blocking collectives: 10 us -> 0 us
    all_gather x2 -> x0, waiting for transfers between devices: 280 us -> none  [the longest x1 141 us: on_device(): lax.all_gather(line_keys, 'ctx', axis=0, tiled=True)]
    gather x5 -> x0, local copies, waits for them, and re-layouts: 133 us -> none  [the longest x1 65.6 us: on_device(): jnp.take_along_axis(key_tiles, gather_index, axis=0)]
    pallas_call x0 -> x1, Pallas kernels: none -> 63.5 us  [on_device(): pl.pallas_call(kernel, out_shape=jax.ShapeDtypeStruct((rows // heads, hea...]
    dot_general x10 -> x0, matrix products: 23.7 us -> none  [the longest x4 13.3 us: absorb(): jnp.einsum('kgtn,nkd->kgtd', weights, piece_values.astype(jnp.float32))]
    all_to_all x1 -> x0, blocking collectives: 10 us -> none  [on_device(): lax.all_to_all(stacked, 'head', split_axis=0, concat_axis=0, tiled=True)]
    reduce_sum x5 -> x0, other arithmetic: 7.45 us -> none  [the longest x4 7.29 us: absorb(): new_sum = sum_now * rescale + jnp.sum(weights, axis=3)]
  transfers between devices with their start and end apart: 2 -> 0, of which waited for: 2 -> 0; matrix products, arithmetic and copies ran while one was open for 1% -> 0% of each run, Pallas kernels for 0% -> 0%
where the time goes in v1:
time: 68.6 us; the launch traced here: 68.2 us
  Pallas kernels  63.5 us (93%)
  local copies, waits for them, and re-layouts  4.77 us (7%)
    pallas_call x1, Pallas kernels, on_device(): pl.pallas_call(kernel, out_shape=jax.ShapeDtypeStruct((rows // heads, hea...  63.5 us
    unnamed x13, local copies, waits for them, and re-layouts  4.77 us

profile of v1, /device:TPU:1, one launch (start us, length us, event | category | flops | bytes accessed | tf_op | source)
XLA Modules:
  0.0 68.2 jit_solution(12346835066970443083)
XLA Ops:
  0.0 0.0 copy-start.4
  0.0 0.0 copy-start.5
  0.0 0.7 copy-done.4
  0.7 0.0 copy-done.5
  0.7 0.0 copy-start
  0.7 0.9 %copy-done = bf16[256,512]{1,0:T(8,128)(2,1)S(1)} copy-done((bf16[256,512]{1,0:T(8,128)(2,1)S(1)}, bf16[256,512]{1,0:T(8,128)(2,1)}, u32[]{:S(2)}) %copy-start) | copy-done | bytes 262168
  1.6 0.0 copy-start.1
  1.6 0.8 %copy-done.1 = bf16[256,128]{1,0:T(8,128)(2,1)S(1)} copy-done((bf16[256,128]{1,0:T(8,128)(2,1)S(1)}, bf16[256,128]{1,0:T(8,128)(2,1)}, u32[]{:S(2)}) %copy-start.1) | copy-done | bytes 65560
  2.5 0.0 copy-start.2
  2.5 0.8 %copy-done.2 = bf16[256,128]{1,0:T(8,128)(2,1)S(1)} copy-done((bf16[256,128]{1,0:T(8,128)(2,1)S(1)}, bf16[256,128]{1,0:T(8,128)(2,1)}, u32[]{:S(2)}) %copy-start.2) | copy-done | bytes 65560
  3.3 0.0 copy-start.3
  3.3 0.8 %copy-done.3 = s32[8192,1]{0,1:T(1,128)S(1)} copy-done((s32[8192,1]{0,1:T(1,128)S(1)}, s32[8192,1]{0,1:T(1,128)}, u32[]{:S(2)}) %copy-start.3) | copy-done | bytes 32792
  4.1 63.5 %shard_map.64 = bf16[64,2048]{1,0:T(8,128)(2,1)S(1)} custom-call(bf16[256,512]{1,0:T(8,128)(2,1)S(1)} %copy-done, bf16[256,128]{1,0:T(8,128)(2,1)S(1)} %copy-done.1, bf16[256,128]{1,0:T(8,128)(2,1)S(1)} %copy-done.2, s32[4,16,128]{2,1,0:T(8,128)S(1)} %bitcast.5, s32[8]{0:T(128)S(1)} %bitcast.7, s32[2,4]{1,0:T(2,128)S(1)} %bitcast.6), custom_call_target="tpu_custom_call" | custom-call | flops 4294967296 | bytes 1048576 | tf_op jit(solution)/shard_map/pallas_call | solution.py:275
  67.5 0.7 %copy.8 = bf16[64,2048]{1,0:T(8,128)(2,1)} copy(bf16[64,2048]{1,0:T(8,128)(2,1)S(1)} %shard_map.64) | data formatting | bytes 524288
Async XLA Ops:
  0.0 0.7 copy-start.4
  0.0 0.7 copy-start.5
  0.7 1.0 %copy-start = (bf16[256,512]{1,0:T(8,128)(2,1)S(1)}, bf16[256,512]{1,0:T(8,128)(2,1)}, u32[]{:S(2)}) copy-start(bf16[256,512]{1,0:T(8,128)(2,1)} %q_hbm.1) | copy-start | bytes 786436
  1.6 0.8 %copy-start.1 = (bf16[256,128]{1,0:T(8,128)(2,1)S(1)}, bf16[256,128]{1,0:T(8,128)(2,1)}, u32[]{:S(2)}) copy-start(bf16[256,128]{1,0:T(8,128)(2,1)} %k_hbm.1) | copy-start | bytes 196612
  2.5 0.8 %copy-start.2 = (bf16[256,128]{1,0:T(8,128)(2,1)S(1)}, bf16[256,128]{1,0:T(8,128)(2,1)}, u32[]{:S(2)}) copy-start(bf16[256,128]{1,0:T(8,128)(2,1)} %v_hbm.1) | copy-start | bytes 196612
  3.3 0.8 %copy-start.3 = (s32[8192,1]{0,1:T(1,128)S(1)}, s32[8192,1]{0,1:T(1,128)}, u32[]{:S(2)}) copy-start(s32[8192,1]{0,1:T(1,128)} %param.9) | copy-start | bytes 98308

commit v2 on v1

--- a/solution.py
+++ b/solution.py
@@ -20,11 +20,27 @@
 MESH = pl.DeviceIdType.MESH
 
 
+TREE = {0: ((4, 4), (1, 1)), 1: ((1, 2),), 2: ((1, 3),), 4: ((2, 6), (1, 5)), 6: ((2, 8), (1, 7))}
+ORDER = (0, -1, 1, -4, 4, -2, 2, -5, 5, -6, 6, -3, 3, -7, 7, 8)
+STEPS = {
+    0: (("own", 2), ("rest", 1)),
+    1: (("own", 5), ("own", 6)),
+    2: (("rest", 4), ("own", 3)),
+    4: (("rest", 2), ("own", 7), ("own", 8)),
+    6: (("rest", 5),),
+    7: (("rest", 6),),
+    9: (("rest", 3),),
+    11: (("rest", 7), ("rest", 8)),
+}
+ROWS = 2 * VB
+SPLIT = 48
+
+
 def kernel(
     q_hbm, k_hbm, v_hbm, vr_hbm, slash_ref, bm_ref, out_hbm,
     q_ref, k_ref, v_ref, vr_ref, lines, peak, acc, res,
-    in_sem, y_send, y_recv, up_send, up_recv, dn_send, dn_recv,
-    su_send, su_recv, sd_send, sd_recv, x_send, x_recv, own_sem,
+    in_sem, a_send, a_recv, b_send, b_recv, y_send, y_recv,
+    s_send, s_recv, x_send, x_recv, own_sem,
 ):
     c = lax.axis_index("ctx")
     h = lax.axis_index("head")
@@ -37,8 +53,13 @@
         return (yy * (NZ * NC) + zz * NC + cc, h)
 
     sibling = dev(y, z, 1 - core)
-    z_up = dev(y, (z + 1) % NZ, core)
-    z_dn = dev(y, (z + NZ - 1) % NZ, core)
+    opposite = (y + 2) % NY
+
+    def along(hop, upward):
+        return (z + hop) % NZ if upward else (z + NZ - hop) % NZ
+
+    def owner_of(distance, upward):
+        return along(distance, not upward)
 
     loads = [
         pltpu.make_async_copy(src, dst, in_sem.at[i])
@@ -50,7 +71,8 @@
         load.start()
 
     barrier = pltpu.get_barrier_semaphore()
-    greeted = [sibling, z_up, z_dn]
+    greeted = [sibling]
+    greeted += [dev(y, along(hop, up), core) for hop in (1, 2, 4) for up in (True, False)]
     greeted += [dev((y + d) % NY, z, core) for d in (1, 2, 3)]
     greeted += [(c, (h + d) % heads) for d in (1, 2, 3)]
     for who in greeted:
@@ -68,48 +90,83 @@
         for cc in range(NC):
             @pl.when(core == cc)
             def _():
-                lines[z, kv, y, cc] = both[cc * VB : (cc + 1) * VB]
+                lines[z, y, cc, kv * VB : (kv + 1) * VB] = both[cc * VB : (cc + 1) * VB]
 
     pl.semaphore_wait(barrier, len(greeted))
 
-    def y_copy(d):
-        block = lines.at[z, :, y, core]
+    def remote(block, send, recv, to):
         return pltpu.make_async_remote_copy(
-            block, block, y_send.at[d - 1], y_recv.at[d - 1],
-            device_id=dev((y + d) % NY, z, core), device_id_type=MESH,
-        )
-
-    for d in (1, 2, 3):
-        y_copy(d).start()
+            block, block, send, recv, device_id=to, device_id_type=MESH
+        )
+
+    def z_copy(kind, held, hop, reached, upward):
+        zz = owner_of(held, upward)
+        send, recv, yy, first = (
+            (a_send, a_recv, y, 0) if kind == "own" else (b_send, b_recv, opposite, SPLIT)
+        )
+        cut = 64 if kind == "own" else 96
+        last = ROWS
+        if reached == 8:
+            first, last = (first, cut) if upward else (cut, ROWS)
+        return remote(
+            lines.at[zz, yy, core, pl.ds(first, last - first)],
+            send.at[int(upward), reached], recv.at[int(upward), reached],
+            dev(y, along(hop, upward), core),
+        )
+
+    def z_sends(kind, held):
+        return [
+            z_copy(kind, held, hop, reached, upward)
+            for hop, reached in TREE.get(held, ())
+            for upward in (True, False)
+        ]
+
+    def z_arrivals(kind, reached):
+        hop, held = next(
+            (hop, held) for held, to in TREE.items() for hop, at in to if at == reached
+        )
+        return [z_copy(kind, held, hop, reached, upward) for upward in (True, False)]
+
+    def y_copy(distance, d):
+        rows = SPLIT if d == 2 and distance != 0 else ROWS
+        return remote(
+            lines.at[(z + NZ + distance) % NZ, y, core, pl.ds(0, rows)],
+            y_send.at[d - 1, distance % NZ], y_recv.at[d - 1, distance % NZ],
+            dev((y + d) % NY, z, core),
+        )
+
+    def s_copy(rel):
+        return remote(
+            lines.at[(z + rel) % NZ, :, core], s_send.at[rel], s_recv.at[rel], sibling
+        )
+
+    def signed(distance):
+        return (0,) if distance == 0 else (8,) if distance == 8 else (-distance, distance)
+
+    def own_step(distance):
+        for copy in z_arrivals("own", distance):
+            copy.wait_recv()
+        for copy in z_sends("own", distance):
+            copy.start()
+        for at in signed(distance):
+            for d in (2, 1, 3):
+                y_copy(at, d).start()
+
+    def rest_step(distance):
+        for copy in z_arrivals("rest", distance):
+            copy.wait_recv()
+        for copy in z_sends("rest", distance):
+            copy.start()
+        for at in signed(distance):
+            for d in (1, 2, 3):
+                y_copy(at, d).wait_recv()
+            s_copy(at % NZ).start()
+
+    for copy in z_sends("own", 0):
+        copy.start()
+    for d in (2, 1, 3):
+        y_copy(0, d).start()
     loads[3].wait()
-
-    def z_copy(s, zz, upward):
-        block = lines.at[zz, :, :, core]
-        if upward:
-            return pltpu.make_async_remote_copy(
-                block, block, up_send.at[s], up_recv.at[s], device_id=z_up, device_id_type=MESH
-            )
-        return pltpu.make_async_remote_copy(
-            block, block, dn_send.at[s], dn_recv.at[s], device_id=z_dn, device_id_type=MESH
-        )
-
-    def last_copy(zz, upward):
-        kv = 0 if upward else 1
-        block = lines.at[zz, kv, :, core]
-        if upward:
-            return pltpu.make_async_remote_copy(
-                block, block, up_send.at[8], up_recv.at[8], device_id=z_up, device_id_type=MESH
-            )
-        return pltpu.make_async_remote_copy(
-            block, block, dn_send.at[8], dn_recv.at[8], device_id=z_dn, device_id_type=MESH
-        )
-
-    def sib_copy(s, zz, upward, who):
-        block = lines.at[zz, :, :, who]
-        send, recv = (su_send, su_recv) if upward else (sd_send, sd_recv)
-        return pltpu.make_async_remote_copy(
-            block, block, send.at[s], recv.at[s], device_id=sibling, device_id_type=MESH
-        )
 
     ones = jnp.ones((NY * NC * VB, HD), jnp.bfloat16)
 
@@ -160,8 +217,8 @@
             owner = yy * (NZ * NC) + zz * NC + lane // VB
             low_bias.append(jnp.where(is_low & (owner < c), 0.0, NEG))
             high_bias.append(jnp.where(is_low | (owner > c), 0.0, NEG))
-        keys = lines[zz, 0].reshape(NY * NC * VB, HD)
-        vals = jnp.concatenate([lines[zz, 1].reshape(NY * NC * VB, HD), ones], axis=1)
+        keys = lines[zz, :, :, :VB].reshape(NY * NC * VB, HD)
+        vals = jnp.concatenate([lines[zz, :, :, VB:].reshape(NY * NC * VB, HD), ones], axis=1)
         for half, parts in ((0, low_bias), (1, high_bias)):
             bias = jnp.concatenate(parts, axis=1)
             s = lax.dot_general(
@@ -178,44 +235,28 @@
                 weights.astype(jnp.bfloat16), vals, preferred_element_type=jnp.float32
             )
 
-    for d in (1, 2, 3):
-        y_copy(d).wait_recv()
-    z_copy(1, z, True).start()
-    z_copy(1, z, False).start()
-    sib_copy(0, z, True, core).start()
-
-    sib_copy(0, z, True, 1 - core).wait_recv()
-    absorb(z)
-
-    def step(s, carry):
-        for upward in (True, False):
-            zz = (z + NZ - s) % NZ if upward else (z + s) % NZ
-            z_copy(s, zz, upward).wait_recv()
-            @pl.when(s < 7)
+    own_step(1)
+    for d in (2, 1, 3):
+        y_copy(0, d).wait_recv()
+    for copy in z_sends("rest", 0):
+        copy.start()
+    s_copy(0).start()
+    own_step(4)
+
+    def chunk(i, carry):
+        for j, todo in STEPS.items():
+            @pl.when(i == j)
             def _():
-                z_copy(s + 1, zz, upward).start()
-            @pl.when(s == 7)
-            def _():
-                last_copy(zz, upward).start()
-            sib_copy(s, zz, upward, core).start()
-            @pl.when(s > 1)
-            def _():
-                before = (z + NZ - s + 1) % NZ if upward else (z + s - 1) % NZ
-                sib_copy(s - 1, before, upward, 1 - core).wait_recv()
-                absorb(before)
+                for kind, distance in todo:
+                    (own_step if kind == "own" else rest_step)(distance)
+        rel = jnp.int32(0)
+        for j, distance in enumerate(ORDER):
+            rel = jnp.where(i == j, distance % NZ, rel)
+        s_copy(rel).wait_recv()
+        absorb((z + rel) % NZ)
         return carry
 
-    lax.fori_loop(1, 8, step, 0)
-    far = (z + 8) % NZ
-    last_copy(far, True).wait_recv()
-    last_copy(far, False).wait_recv()
-    sib_copy(8, far, True, core).start()
-    for upward in (True, False):
-        before = (z + NZ - 7) % NZ if upward else (z + 7) % NZ
-        sib_copy(7, before, upward, 1 - core).wait_recv()
-        absorb(before)
-    sib_copy(8, far, True, 1 - core).wait_recv()
-    absorb(far)
+    lax.fori_loop(0, NZ, chunk, 0)
 
     quarter = res.shape[0] // 4
     cols = GROUP * HD
@@ -245,21 +286,19 @@
     for d in (2, 1, 3):
         x_copy(d).start()
 
-    for d in (1, 2, 3):
-        y_copy(d).wait_send()
-    sib_copy(0, z, True, core).wait_send()
-
-    def drain(s, carry):
-        for upward in (True, False):
-            zz = (z + NZ - s) % NZ if upward else (z + s) % NZ
-            z_copy(s, zz, upward).wait_send()
-            sib_copy(s, zz, upward, core).wait_send()
+    for kind in ("own", "rest"):
+        for held in TREE:
+            for copy in z_sends(kind, held):
+                copy.wait_send()
+    for distance in ORDER:
+        for d in (1, 2, 3):
+            y_copy(distance, d).wait_send()
+
+    def drain(rel, carry):
+        s_copy(rel).wait_send()
         return carry
 
-    lax.fori_loop(1, 8, drain, 0)
-    last_copy(far, True).wait_send()
-    last_copy(far, False).wait_send()
-    sib_copy(8, far, True, core).wait_send()
+    lax.fori_loop(0, NZ, drain, 0)
     own.wait()
     for d in (1, 2, 3):
         x_copy(d).wait_send()
@@ -275,7 +314,7 @@
     return pl.pallas_call(
         kernel,
         out_shape=jax.ShapeDtypeStruct((rows // heads, heads * cols), jnp.bfloat16),
-        in_specs=[pl.BlockSpec(memory_space=pl.ANY)] * 4
+        in_specs=[pl.BlockSpec(memory_space=pltpu.HBM)] * 4
         + [pl.BlockSpec(memory_space=pltpu.SMEM)] * 2,
         out_specs=pl.BlockSpec(memory_space=pl.ANY),
         scratch_shapes=[
@@ -283,19 +322,19 @@
             pltpu.VMEM((rows, HD), jnp.bfloat16),
             pltpu.VMEM((rows, HD), jnp.bfloat16),
             pltpu.VMEM((NY, NZ, NC * VB), jnp.int32),
-            pltpu.VMEM((NZ, 2, NY, NC, VB, HD), jnp.bfloat16),
+            pltpu.VMEM((NZ, NY, NC, ROWS, HD), jnp.bfloat16),
             pltpu.VMEM((2, GROUP * HALF, HD), jnp.float32),
             pltpu.VMEM((2, GROUP * HALF, 2 * HD), jnp.float32),
             pltpu.VMEM((rows, cols), jnp.bfloat16),
             dma((4,)),
-            dma((3,)), dma((3,)),
-            dma((9,)), dma((9,)), dma((9,)), dma((9,)),
-            dma((9,)), dma((9,)), dma((9,)), dma((9,)),
+            dma((2, 9)), dma((2, 9)), dma((2, 9)), dma((2, 9)),
+            dma((3, NZ)), dma((3, NZ)),
+            dma((NZ,)), dma((NZ,)),
             dma((3,)), dma((3,)),
             dma,
         ],
         compiler_params=pltpu.CompilerParams(
-            collective_id=0, has_side_effects=True, vmem_limit_bytes=48 * 1024 * 1024
+            collective_id=0, has_side_effects=True, vmem_limit_bytes=60 * 1024 * 1024
         ),
         cost_estimate=pl.CostEstimate(
             flops=4 * 1024 * 8192 * HD, bytes_accessed=2**20, transcendentals=1024 * 8192

time: 68.6 us -> 55.2 us (0.80)
  Pallas kernels: 63.5 us -> 53.4 us
  local copies, waits for them, and re-layouts: 4.77 us -> 1.67 us
    pallas_call x1, Pallas kernels: 63.5 us -> 53.4 us  [on_device(): pl.pallas_call(kernel, out_shape=jax.ShapeDtypeStruct((rows // heads, hea...]
    unnamed x13 -> x1, local copies, waits for them, and re-layouts: 4.77 us -> 1.67 us
where the time goes in v2:
time: 55.2 us; the launch traced here: 55 us
  Pallas kernels  53.4 us (97%)
  local copies, waits for them, and re-layouts  1.67 us (3%)
    pallas_call x1, Pallas kernels, on_device(): pl.pallas_call(kernel, out_shape=jax.ShapeDtypeStruct((rows // heads, hea...  53.4 us
    unnamed x1, local copies, waits for them, and re-layouts  1.67 us

profile of v2, /device:TPU:1, one launch (start us, length us, event | category | flops | bytes accessed | tf_op | source)
XLA Modules:
  0.0 55.0 jit_solution(12154676008771218801)
XLA Ops:
  0.0 53.4 %shard_map.64 = bf16[64,2048]{1,0:T(8,128)(2,1)} custom-call(bf16[256,512]{1,0:T(8,128)(2,1)} %q_hbm.1, bf16[256,128]{1,0:T(8,128)(2,1)} %k_hbm.1, bf16[256,128]{1,0:T(8,128)(2,1)} %v_hbm.1, s32[4,16,128]{2,1,0:T(8,128)} %bitcast.5, s32[8]{0:T(128)} %bitcast.7, s32[2,4]{1,0:T(2,128)} %bitcast.6), custom_call_target="tpu_custom_call" | custom-call | flops 4294967296 | bytes 1048576 | tf_op jit(solution)/shard_map/pallas_call | solution.py:314
  53.4 1.7 %copy.8 = bf16[64,2048]{1,0:T(8,128)(2,1)} copy(bf16[64,2048]{1,0:T(8,128)(2,1)} %shard_map.64) | data formatting | bytes 524288

commit v3 on v2

--- a/solution.py
+++ b/solution.py
@@ -20,25 +20,29 @@
 MESH = pl.DeviceIdType.MESH
 
 
-TREE = {0: ((4, 4), (1, 1)), 1: ((1, 2),), 2: ((1, 3),), 4: ((2, 6), (1, 5)), 6: ((2, 8), (1, 7))}
-ORDER = (0, -1, 1, -4, 4, -2, 2, -5, 5, -6, 6, -3, 3, -7, 7, 8)
+TREE = {0: ((2, 2), (1, 1)), 2: ((2, 4), (1, 3)), 4: ((2, 6), (1, 5)), 6: ((2, 8), (1, 7))}
+HOPS = (2, 1)
+PAIRS = (1, 2, 3, 4, 5, 6)
+LAST = 7
+FIRST = (("own", 1), ("own", 2), ("first", 0))
+EARLY = (("rest", 1), ("own", 4), ("own", 3), ("rest", 2))
 STEPS = {
-    0: (("own", 2), ("rest", 1)),
-    1: (("own", 5), ("own", 6)),
-    2: (("rest", 4), ("own", 3)),
-    4: (("rest", 2), ("own", 7), ("own", 8)),
+    1: (("own", 6), ("own", 5)),
+    2: (("rest", 4),),
+    3: (("rest", 3),),
+    4: (("own", 8), ("own", 7)),
+    5: (("rest", 6),),
     6: (("rest", 5),),
-    7: (("rest", 6),),
-    9: (("rest", 3),),
-    11: (("rest", 7), ("rest", 8)),
+    8: (("rest", 8),),
+    9: (("rest", 7),),
 }
 ROWS = 2 * VB
-SPLIT = 48
+SPLIT = 32
 
 
 def kernel(
     q_hbm, k_hbm, v_hbm, vr_hbm, slash_ref, bm_ref, out_hbm,
-    q_ref, k_ref, v_ref, vr_ref, lines, peak, acc, res,
+    q_ref, k_ref, v_ref, vr_ref, lines, bias_ref, peak, acc, res,
     in_sem, a_send, a_recv, b_send, b_recv, y_send, y_recv,
     s_send, s_recv, x_send, x_recv, own_sem,
 ):
@@ -64,17 +68,25 @@
     loads = [
         pltpu.make_async_copy(src, dst, in_sem.at[i])
         for i, (src, dst) in enumerate(
-            ((vr_hbm, vr_ref), (k_hbm, k_ref), (v_hbm, v_ref), (q_hbm, q_ref))
+            [(vr_hbm, vr_ref), (k_hbm, k_ref), (v_hbm, v_ref)]
+            + [
+                (
+                    q_hbm.at[pl.ds(half * HALF, HALF), pl.ds(g * HD, HD)],
+                    q_ref.at[half * GROUP + g],
+                )
+                for half in range(2)
+                for g in range(GROUP)
+            ]
         )
     ]
     for load in loads:
         load.start()
 
     barrier = pltpu.get_barrier_semaphore()
-    greeted = [sibling]
-    greeted += [dev(y, along(hop, up), core) for hop in (1, 2, 4) for up in (True, False)]
+    greeted = [dev(y, along(hop, up), core) for hop in HOPS for up in (True, False)]
     greeted += [dev((y + d) % NY, z, core) for d in (1, 2, 3)]
     greeted += [(c, (h + d) % heads) for d in (1, 2, 3)]
+    greeted += [sibling]
     for who in greeted:
         pl.semaphore_signal(barrier, inc=1, device_id=who, device_id_type=MESH)
 
@@ -166,18 +178,23 @@
         copy.start()
     for d in (2, 1, 3):
         y_copy(0, d).start()
-    loads[3].wait()
 
     ones = jnp.ones((NY * NC * VB, HD), jnp.bfloat16)
 
-    def queries_of(half):
-        return jnp.concatenate(
-            [
-                q_ref[half * HALF : (half + 1) * HALF, g * HD : (g + 1) * HD]
-                for g in range(GROUP)
-            ],
-            axis=0,
-        )
+    owner = (
+        lax.broadcasted_iota(jnp.int32, (NZ, NC * VB), 0) * NC
+        + lax.broadcasted_iota(jnp.int32, (NZ, NC * VB), 1) // VB
+    )
+    for yy in range(NY):
+        is_low = vr_ref[yy] < HALF
+        at = slice(yy * NC * VB, (yy + 1) * NC * VB)
+        before = owner + yy * (NZ * NC) < c
+        after = owner + yy * (NZ * NC) > c
+        bias_ref[0, :, at] = jnp.where(is_low & before, 0.0, NEG)
+        bias_ref[1, :, at] = jnp.where(is_low | after, 0.0, NEG)
+
+    for load in loads[3:]:
+        load.wait()
 
     qi = lax.broadcasted_iota(jnp.int32, (HALF, HALF), 0)
     kj = lax.broadcasted_iota(jnp.int32, (HALF, HALF), 1)
@@ -197,100 +214,138 @@
         allowed = (kj <= qi) & (base | hit)
         bias = jnp.where(allowed, 0.0, NEG)
         rows = slice(half * HALF, (half + 1) * HALF)
-        s = lax.dot_general(
-            queries_of(half), k_ref[rows, :], (((1,), (1,)), ((), ())),
-            preferred_element_type=jnp.float32,
-        )
-        s = s + jnp.concatenate([bias] * GROUP, axis=0)
-        top_score = jnp.broadcast_to(jnp.max(s, axis=1, keepdims=True), s.shape)
-        peak[half] = top_score
-        weights = jnp.exp2((s - top_score) * SCALE).astype(jnp.bfloat16)
         vals = jnp.concatenate([v_ref[rows, :], ones[:HALF]], axis=1)
-        acc[half] = jnp.dot(weights, vals, preferred_element_type=jnp.float32)
-
-    lane = lax.broadcasted_iota(jnp.int32, (1, NC * VB), 1)
-
-    def absorb(zz):
-        low_bias, high_bias = [], []
-        for yy in range(NY):
-            is_low = vr_ref[yy, pl.ds(zz, 1), :] < HALF
-            owner = yy * (NZ * NC) + zz * NC + lane // VB
-            low_bias.append(jnp.where(is_low & (owner < c), 0.0, NEG))
-            high_bias.append(jnp.where(is_low | (owner > c), 0.0, NEG))
-        keys = lines[zz, :, :, :VB].reshape(NY * NC * VB, HD)
-        vals = jnp.concatenate([lines[zz, :, :, VB:].reshape(NY * NC * VB, HD), ones], axis=1)
-        for half, parts in ((0, low_bias), (1, high_bias)):
-            bias = jnp.concatenate(parts, axis=1)
+        for t in range(half * GROUP, (half + 1) * GROUP):
             s = lax.dot_general(
-                queries_of(half), keys, (((1,), (1,)), ((), ())),
+                q_ref[t], k_ref[rows, :], (((1,), (1,)), ((), ())),
                 preferred_element_type=jnp.float32,
             )
             s = s + bias
-            old = peak[half]
+            top_score = jnp.broadcast_to(jnp.max(s, axis=1, keepdims=True), s.shape)
+            peak[t] = top_score
+            weights = jnp.exp2((s - top_score) * SCALE).astype(jnp.bfloat16)
+            acc[t] = jnp.dot(weights, vals, preferred_element_type=jnp.float32)
+
+    def absorb(half, chunks):
+        def all_keys(first):
+            return jnp.concatenate(
+                [lines[zz, :, :, first : first + VB].reshape(NY * NC * VB, HD) for zz in chunks],
+                axis=0,
+            )
+
+        keys = all_keys(0)
+        vals = jnp.concatenate(
+            [all_keys(VB), jnp.concatenate([ones] * len(chunks), axis=0)], axis=1
+        )
+        bias = jnp.concatenate([bias_ref[half, pl.ds(zz, 1), :] for zz in chunks], axis=1)
+        scores = [
+            lax.dot_general(
+                q_ref[half * GROUP + g], keys, (((1,), (1,)), ((), ())),
+                preferred_element_type=jnp.float32,
+            )
+            + bias
+            for g in range(GROUP)
+        ]
+        for g in range(GROUP):
+            t = half * GROUP + g
+            s = scores[g]
+            old = peak[t]
             new = jnp.maximum(old, jnp.max(s, axis=1, keepdims=True))
-            peak[half] = new
-            weights = jnp.exp2((s - jnp.concatenate([new] * NY, axis=1)) * SCALE)
+            peak[t] = new
+            weights = jnp.exp2((s - jnp.concatenate([new] * (NY * len(chunks)), axis=1)) * SCALE)
             rescale = jnp.exp2((old - new) * SCALE)
-            acc[half] = acc[half] * jnp.concatenate([rescale] * 2, axis=1) + jnp.dot(
+            acc[t] = acc[t] * jnp.concatenate([rescale] * 2, axis=1) + jnp.dot(
                 weights.astype(jnp.bfloat16), vals, preferred_element_type=jnp.float32
             )
 
-    own_step(1)
-    for d in (2, 1, 3):
-        y_copy(0, d).wait_recv()
-    for copy in z_sends("rest", 0):
-        copy.start()
-    s_copy(0).start()
-    own_step(4)
-
-    def chunk(i, carry):
+    def first_step(distance):
+        for d in (2, 1, 3):
+            y_copy(distance, d).wait_recv()
+        for copy in z_sends("rest", distance):
+            copy.start()
+        s_copy(distance).start()
+
+    def do(todo):
+        for kind, distance in todo:
+            {"own": own_step, "rest": rest_step, "first": first_step}[kind](distance)
+
+    do(FIRST)
+
+    def near(half, carry):
+        absorb(half, [z])
+        return carry
+
+    s_copy(0).wait_recv()
+    lax.fori_loop(0, 2, near, 0)
+
+    do(EARLY)
+
+    def pair(u, carry):
+        half = u % 2
         for j, todo in STEPS.items():
-            @pl.when(i == j)
+            @pl.when(u == j)
             def _():
-                for kind, distance in todo:
-                    (own_step if kind == "own" else rest_step)(distance)
-        rel = jnp.int32(0)
-        for j, distance in enumerate(ORDER):
-            rel = jnp.where(i == j, distance % NZ, rel)
+                do(todo)
+        distance = jnp.int32(0)
+        for j, at in enumerate(PAIRS):
+            distance = jnp.where(u // 2 == j, at, distance)
+
+        @pl.when(half == 0)
+        def _():
+            s_copy(NZ - distance).wait_recv()
+            s_copy(distance).wait_recv()
+
+        chunks = [(z + NZ - distance) % NZ, (z + distance) % NZ]
+
+        @pl.when((half == 1) | (jnp.minimum(chunks[0], chunks[1]) * NC < c))
+        def _():
+            absorb(half, chunks)
+        return carry
+
+    lax.fori_loop(0, 2 * len(PAIRS), pair, 0)
+    for rel in (NZ - LAST, LAST, 8):
         s_copy(rel).wait_recv()
-        absorb((z + rel) % NZ)
-        return carry
-
-    lax.fori_loop(0, NZ, chunk, 0)
 
     quarter = res.shape[0] // 4
     cols = GROUP * HD
 
-    def x_copy(d):
-        to = (h + d) % heads
+    def x_copy(to, whose):
         return pltpu.make_async_remote_copy(
             res.at[pl.ds(to * quarter, quarter), :],
             out_hbm.at[:, pl.ds(pl.multiple_of(h * cols, cols), cols)],
-            x_send.at[d - 1], x_recv.at[d - 1],
+            x_send.at[to], x_recv.at[whose],
             device_id=(c, to), device_id_type=MESH,
         )
 
-    for half in range(2):
-        total = acc[half]
-        done = (total[:, :HD] / total[:, HD:]).astype(jnp.bfloat16)
-        for g in range(GROUP):
-            res[half * HALF : (half + 1) * HALF, g * HD : (g + 1) * HD] = done[
-                g * HALF : (g + 1) * HALF
-            ]
     own = pltpu.make_async_copy(
         res.at[pl.ds(h * quarter, quarter), :],
         out_hbm.at[:, pl.ds(pl.multiple_of(h * cols, cols), cols)],
         own_sem,
     )
-    own.start()
-    for d in (2, 1, 3):
-        x_copy(d).start()
+
+    def finish(half, carry):
+        absorb(half, [(z + rel) % NZ for rel in (NZ - LAST, LAST, 8)])
+        rows = pl.ds(pl.multiple_of(half * HALF, HALF), HALF)
+        for g in range(GROUP):
+            total = acc[half * GROUP + g]
+            res[rows, g * HD : (g + 1) * HD] = (total[:, :HD] / total[:, HD:]).astype(jnp.bfloat16)
+        for part in range(2):
+            to = half * 2 + part
+            @pl.when(to == h)
+            def _():
+                own.start()
+            @pl.when(to != h)
+            def _():
+                x_copy(to, h).start()
+        return carry
+
+    lax.fori_loop(0, 2, finish, 0)
 
     for kind in ("own", "rest"):
         for held in TREE:
             for copy in z_sends(kind, held):
                 copy.wait_send()
-    for distance in ORDER:
+    for distance in range(NZ):
         for d in (1, 2, 3):
             y_copy(distance, d).wait_send()
 
@@ -300,10 +355,11 @@
 
     lax.fori_loop(0, NZ, drain, 0)
     own.wait()
-    for d in (1, 2, 3):
-        x_copy(d).wait_send()
-    for d in (1, 2, 3):
-        x_copy(d).wait_recv()
+    for to in range(4):
+        @pl.when(to != h)
+        def _():
+            x_copy(to, to).wait_send()
+            x_copy(to, to).wait_recv()
 
 
 def on_device(queries, key_rows, value_rows, vertical_rows, slash_offsets, block_mask):
@@ -318,19 +374,20 @@
         + [pl.BlockSpec(memory_space=pltpu.SMEM)] * 2,
         out_specs=pl.BlockSpec(memory_space=pl.ANY),
         scratch_shapes=[
-            pltpu.VMEM((rows, cols), jnp.bfloat16),
+            pltpu.VMEM((2 * GROUP, HALF, HD), jnp.bfloat16),
             pltpu.VMEM((rows, HD), jnp.bfloat16),
             pltpu.VMEM((rows, HD), jnp.bfloat16),
             pltpu.VMEM((NY, NZ, NC * VB), jnp.int32),
             pltpu.VMEM((NZ, NY, NC, ROWS, HD), jnp.bfloat16),
-            pltpu.VMEM((2, GROUP * HALF, HD), jnp.float32),
-            pltpu.VMEM((2, GROUP * HALF, 2 * HD), jnp.float32),
+            pltpu.VMEM((2, NZ, NY * NC * VB), jnp.float32),
+            pltpu.VMEM((2 * GROUP, HALF, HD), jnp.float32),
+            pltpu.VMEM((2 * GROUP, HALF, 2 * HD), jnp.float32),
             pltpu.VMEM((rows, cols), jnp.bfloat16),
-            dma((4,)),
+            dma((3 + 2 * GROUP,)),
             dma((2, 9)), dma((2, 9)), dma((2, 9)), dma((2, 9)),
             dma((3, NZ)), dma((3, NZ)),
             dma((NZ,)), dma((NZ,)),
-            dma((3,)), dma((3,)),
+            dma((4,)), dma((4,)),
             dma,
         ],
         compiler_params=pltpu.CompilerParams(

time: 55.2 us -> 49.1 us (0.89)
  the two profiles are of different devices: /device:TPU:1 before, /device:TPU:8 now
where the time goes in v3:
time: 49.1 us; the launch traced here: 48.9 us
  Pallas kernels  47.2 us (96%)
  local copies, waits for them, and re-layouts  1.67 us (3%)
    pallas_call x1, Pallas kernels, on_device(): pl.pallas_call(kernel, out_shape=jax.ShapeDtypeStruct((rows // heads, hea...  47.2 us
    unnamed x1, local copies, waits for them, and re-layouts  1.67 us

profile of v3, /device:TPU:8, one launch (start us, length us, event | category | flops | bytes accessed | tf_op | source)
XLA Modules:
  0.0 48.9 jit_solution(134188408133762848)
XLA Ops:
  0.0 47.2 %shard_map.64 = bf16[64,2048]{1,0:T(8,128)(2,1)} custom-call(bf16[256,512]{1,0:T(8,128)(2,1)} %q_hbm.1, bf16[256,128]{1,0:T(8,128)(2,1)} %k_hbm.1, bf16[256,128]{1,0:T(8,128)(2,1)} %v_hbm.1, s32[4,16,128]{2,1,0:T(8,128)} %bitcast.5, s32[8]{0:T(128)} %bitcast.7, s32[2,4]{1,0:T(2,128)} %bitcast.6), custom_call_target="tpu_custom_call" | custom-call | flops 4294967296 | bytes 1048576 | tf_op jit(solution)/shard_map/pallas_call | solution.py:370
  47.2 1.7 %copy.8 = bf16[64,2048]{1,0:T(8,128)(2,1)} copy(bf16[64,2048]{1,0:T(8,128)(2,1)} %shard_map.64) | data formatting | bytes 524288

commit v4 on v3

--- a/solution.py
+++ b/solution.py
@@ -37,7 +37,7 @@
     9: (("rest", 7),),
 }
 ROWS = 2 * VB
-SPLIT = 32
+SPLIT = 64
 
 
 def kernel(

time: 49.1 us -> 48.7 us (level)
  no operation moved by 1% of the time
where the time goes in v4:
time: 48.7 us; the launch traced here: 48.5 us
  Pallas kernels  46.8 us (96%)
  local copies, waits for them, and re-layouts  1.67 us (3%)
    pallas_call x1, Pallas kernels, on_device(): pl.pallas_call(kernel, out_shape=jax.ShapeDtypeStruct((rows // heads, hea...  46.8 us
    unnamed x1, local copies, waits for them, and re-layouts  1.67 us

profile of v4, /device:TPU:8, one launch (start us, length us, event | category | flops | bytes accessed | tf_op | source)
XLA Modules:
  0.0 48.5 jit_solution(8502248352954494667)
XLA Ops:
  0.0 46.8 %shard_map.64 = bf16[64,2048]{1,0:T(8,128)(2,1)} custom-call(bf16[256,512]{1,0:T(8,128)(2,1)} %q_hbm.1, bf16[256,128]{1,0:T(8,128)(2,1)} %k_hbm.1, bf16[256,128]{1,0:T(8,128)(2,1)} %v_hbm.1, s32[4,16,128]{2,1,0:T(8,128)} %bitcast.5, s32[8]{0:T(128)} %bitcast.7, s32[2,4]{1,0:T(2,128)} %bitcast.6), custom_call_target="tpu_custom_call" | custom-call | flops 4294967296 | bytes 1048576 | tf_op jit(solution)/shard_map/pallas_call | solution.py:370
  46.8 1.7 %copy.8 = bf16[64,2048]{1,0:T(8,128)(2,1)} copy(bf16[64,2048]{1,0:T(8,128)(2,1)} %shard_map.64) | data formatting | bytes 524288
